TPU v7x, 128 devices: a whole 4x4x4 slice. The times are simulated.
128 devices in a mesh: dom: 16 (over y, z), inner: 8 (over x, core).
Axes of the slice: x: 4, y: 4, z: 4, core: 2. Of those that a mesh axis runs over, the one named last changes fastest.
Arguments:
- start_field: float32 [128, 256, 8, 128], P('dom', 'inner'), may hold values from -1.5 to 1.5, as said below
- source_field: float32 [128, 256, 8, 128], P('dom', 'inner'), may hold values from -5 to 5, as said below
- coefficients: float32 [3, 16, 32, 128], P(None, 'dom', 'inner'), may hold values from 0.3 to 3
- outflow: int32 [128, 256], P('dom', 'inner'), may hold values from 0 to 1, as said below
Outputs:
- solution_field: float32 [128, 256, 8, 128], P('dom', 'inner')
- residual: float32 [128, 256, 8, 128], P('dom', 'inner')
Inputs may be any that keep to these rules, and one draw needn't show every extreme that they name: `start_field`: Continuous: all copies of a shared node hold the same value. `source_field`: Continuous: all copies of a shared node hold the same value. A node column is 1 where any element column holding it is an outflow column; all copies of a shared node column agree.
All inputs are finite; a program needn't handle non-finite values.
Results may differ from a plain program's by a relative error of at most 0.0003.
Values sent between devices are 32-bit elements; how exact they have to be, the bound alone decides.
No kernel may reach another device: no remote copies, remote signals or barrier semaphores. Data moves between devices by JAX's collectives and lax.ppermute only.
A program may use at most 64 MiB of HBM per device.

v0:
```python
import functools
import math

import jax
import jax.numpy as jnp
import ml_dtypes
import numpy as np
from jax import lax
from jax.experimental import pallas as pl
from jax.experimental.pallas import tpu as pltpu
from jax.sharding import PartitionSpec as P

INTERIOR_POINTS = (
    -0.8717401485096066,
    -0.5917001814331423,
    -0.2092992179024789,
    0.2092992179024789,
    0.5917001814331423,
    0.8717401485096066,
)
F32 = jnp.float32
BF16 = jnp.bfloat16
VMEM_BYTES = 48 * 1024 * 1024


def legendre_seven(points):
    previous = points * 0.0 + 1.0
    current = points.copy()
    for degree in range(1, 7):
        following = ((2 * degree + 1) * points * current - degree * previous) / (degree + 1)
        previous = current
        current = following
    return current


def jacobi_eigen(matrix):
    extent = matrix.shape[0]
    current = matrix.copy()
    vectors = np.eye(extent)
    for sweep_number in range(12):
        for first_index in range(extent):
            for second_index in range(first_index + 1, extent):
                angle = 0.5 * math.atan2(
                    2.0 * float(current[first_index, second_index]),
                    float(current[second_index, second_index] - current[first_index, first_index]),
                )
                cosine = math.cos(angle)
                sine = math.sin(angle)
                rotation = np.eye(extent)
                rotation[first_index, first_index] = cosine
                rotation[second_index, second_index] = cosine
                rotation[first_index, second_index] = sine
                rotation[second_index, first_index] = -sine
                current = rotation.T @ current @ rotation
                vectors = vectors @ rotation
    return (np.array([float(current[index, index]) for index in range(extent)]), vectors)


def quadrature_tables():
    grid_points = np.array((-1.0,) + INTERIOR_POINTS + (1.0,))
    end_values = legendre_seven(grid_points)
    weights = 2.0 / (56.0 * end_values**2)
    derivative = np.zeros((8, 8))
    for row_index in range(8):
        for column_index in range(8):
            if row_index != column_index:
                derivative[row_index, column_index] = end_values[row_index] / (
                    end_values[column_index] * (grid_points[row_index] - grid_points[column_index])
                )
    derivative[0, 0] = -14.0
    derivative[7, 7] = 14.0
    stiffness = derivative.T @ (weights[:, None] * derivative)
    three_stiffness = np.zeros((22, 22))
    three_mass = np.zeros(22)
    for element_index in range(3):
        element_offset = 7 * element_index
        three_stiffness[
            element_offset : element_offset + 8, element_offset : element_offset + 8
        ] += stiffness
        three_mass[element_offset : element_offset + 8] += weights
    inverse_root = 1.0 / np.sqrt(three_mass[6:16])
    symmetric = inverse_root[:, None] * three_stiffness[6:16, 6:16] * inverse_root[None, :]
    eigen_values, eigen_vectors = jacobi_eigen(symmetric)
    eigen_basis = inverse_root[:, None] * eigen_vectors
    return tuple(
        table.astype(np.float32).astype(np.float64)
        for table in (stiffness, weights, eigen_basis, eigen_values)
    )


STIFF, WEIGHT, BASIS, EIGEN = quadrature_tables()
PARITY = [1.0 if BASIS[0, p] * BASIS[9, p] > 0 else -1.0 for p in range(10)]
HALF_BASIS = np.array(
    [[0.5 * (BASIS[a, p] + PARITY[p] * BASIS[9 - a, p]) for p in range(10)] for a in range(5)]
)
EVEN = [p for p in range(10) if PARITY[p] > 0]
ODD = [p for p in range(10) if PARITY[p] < 0]


def two_parts(matrix):
    high = matrix.astype(ml_dtypes.bfloat16)
    low = (matrix - high.astype(np.float64)).astype(ml_dtypes.bfloat16)
    return high, low


def operator_tables():
    along_second = np.kron(STIFF, np.diag(WEIGHT))
    along_third = np.kron(np.diag(WEIGHT), STIFF)
    sets = []
    for places in (range(8), (0, 1, 6, 7)):
        rows = [8 * j + k for j in places for k in range(8)]
        high, low = two_parts(np.concatenate([along_second[rows], along_third[rows]]))
        sets.append(np.concatenate([high, high, low], axis=1))
    return sets


def transform_tables():
    forward = np.zeros((112, 240))
    backward = np.zeros((160, 112))
    second = BASIS.T
    third = np.zeros((3, 10, 8))
    third[0] = BASIS[1:9].T
    third[1][:, 7] = BASIS[1]
    third[1][:, 6] = BASIS[0]
    third[2][:, 0] = BASIS[8]
    third[2][:, 1] = BASIS[9]
    for group in range(3):
        forward[:100, 80 * group : 80 * group + 80] = np.kron(second, third[group])
    backward[:80, :100] = np.kron(BASIS, BASIS[1:9])
    back_third = np.zeros((8, 10))
    back_third[6] = BASIS[0]
    back_third[7] = BASIS[1]
    back_third[0] = BASIS[8]
    back_third[1] = BASIS[9]
    backward[80:, :100] = np.kron(BASIS, back_third)
    forward_high, forward_low = two_parts(forward)
    back_high, back_low = two_parts(backward)
    second_values = np.ones((112, 128), np.float32)
    third_values = np.ones((112, 128), np.float32)
    second_values[:100] = np.repeat(EIGEN, 10)[:, None]
    third_values[:100] = np.tile(EIGEN, 10)[:, None]
    return (
        forward_high,
        forward_low,
        np.concatenate([back_high, back_high], axis=1),
        back_low,
        second_values,
        third_values,
    )


OPERATOR_OWN, OPERATOR_SIDE = operator_tables()
PLANE_WEIGHTS = np.broadcast_to(
    (WEIGHT[:, None] * WEIGHT[None, :])[:, :, None], (8, 8, 128)
).astype(np.float32)
TRANSFORMS = transform_tables()


def lane_ids():
    return lax.broadcasted_iota(jnp.int32, (8, 128), 1)


def row_ids():
    return lax.broadcasted_iota(jnp.int32, (8, 128), 0)


def split(values):
    high = values.astype(BF16)
    return high, (values - high.astype(F32)).astype(BF16)


def dot(left, right):
    return jnp.dot(left, right, preferred_element_type=F32)


def top_flags():
    return ((lane_ids() == 127) & (row_ids() == 7)).astype(F32)


def own_keep(outflow, top, i, column):
    return 1.0 - outflow[i, column].astype(F32) * top


def spread_row(row):
    return jnp.broadcast_to(row, (8, 128))


def pack_body(start_low, start_high, source_low, source_high, coefficients, outflow, low, high):
    top = top_flags()
    rows = row_ids()
    for target, start, source, first, node, element in (
        (low, start_low, source_low, 1, 1, 0),
        (high, start_high, source_high, 0, 6, 3),
    ):
        gains = [spread_row(coefficients[c, 0, element : element + 1, :]) for c in range(3)]
        for i in range(8):
            target[i, 0:7] = start[i, first : first + 7]
            target[i, 7] = source[i, node]
            keep = own_keep(outflow, top, i, 8 * element + node)
            info = jnp.where(rows == 0, gains[0], jnp.where(rows == 1, gains[1], gains[2]))
            target[i, 8] = jnp.where(rows == 7, keep, info)


def pack_first(start, source, coefficients, outflow):
    low_block = pl.BlockSpec((8, 8, 8, 128), lambda g: (0, 0, 0, 0))
    high_block = pl.BlockSpec((8, 8, 8, 128), lambda g: (0, 3, 0, 0))
    shape = jax.ShapeDtypeStruct((8, 9, 8, 128), F32)
    return pl.pallas_call(
        pack_body,
        grid=(1,),
        out_shape=(shape, shape),
        in_specs=[
            low_block,
            high_block,
            low_block,
            high_block,
            pl.BlockSpec((3, 1, 4, 128), lambda g: (0, 0, 0, 0)),
            pl.BlockSpec(memory_space=pltpu.SMEM),
        ],
        out_specs=(
            pl.BlockSpec((8, 9, 8, 128), lambda g: (0, 0, 0, 0)),
            pl.BlockSpec((8, 9, 8, 128), lambda g: (0, 0, 0, 0)),
        ),
        name="pack_first",
    )(start, start, source, source, coefficients, outflow)


def first_direction(values):
    sums = [values[a] + values[7 - a] for a in range(4)]
    gaps = [values[a] - values[7 - a] for a in range(4)]
    outs = [None] * 8
    for i in range(4):
        even = odd = None
        for a in range(4):
            even_term = sums[a] * float(0.5 * (STIFF[i, a] + STIFF[i, 7 - a]))
            odd_term = gaps[a] * float(0.5 * (STIFF[i, a] - STIFF[i, 7 - a]))
            even = even_term if even is None else even + even_term
            odd = odd_term if odd is None else odd + odd_term
        outs[i] = even + odd
        outs[7 - i] = even - odd
    return outs


def residual_part(field, gains, own_table, side_table, plane_weights, planes, image):
    def products(pair, table, count):
        def step(i, carry):
            values = jnp.concatenate(
                [field[i, 7 * e : 7 * e + 8].reshape(64, 128) for e in pair], axis=1
            )
            high, low = split(values)
            planes[i, 0:count] = dot(table[...], jnp.concatenate([high, low, high], axis=0))
            return carry

        lax.fori_loop(0, 8, step, 0)

    def combine(e, lane, j, second_at, third_at, target, add):
        gain = gains(e)
        terms = first_direction([field[a, 7 * e + j] for a in range(8)])
        plane = gain[0] * plane_weights[j]
        for i in range(8):
            second = planes[i, pl.ds(second_at, 8), lane]
            third = planes[i, pl.ds(third_at, 8), lane]
            value = plane * terms[i] + float(WEIGHT[i]) * (gain[1] * second + gain[2] * third)
            if add:
                value = value + image[i, target]
            image[i, target] = value

    lanes = (slice(0, 128), slice(128, 256))
    products((0, 5), side_table, 64)
    for q in range(2):
        combine(0, lanes[0], 6 + q, 16 + 8 * q, 48 + 8 * q, q, False)
        combine(5, lanes[1], q, 8 * q, 32 + 8 * q, 29 + q, False)
    for pair in ((1, 2), (3, 4)):
        products(pair, own_table, 128)
        for e, lane in zip(pair, lanes):
            base = 7 * (e - 1) + 1
            combine(e, lane, 0, 0, 64, base, True)

            def step(j, carry, e=e, lane=lane, base=base):
                at = pl.multiple_of(8 * j, 8)
                combine(e, lane, j, at, at + 64, base + j, False)
                return carry

            lax.fori_loop(1, 7, step, 0)
            combine(e, lane, 7, 56, 120, base + 7, e == 4)


def gains_of(coefficients, from_low, from_high):
    def gains(e):
        if e == 0:
            return [spread_row(from_low[0, 8, c : c + 1, :]) for c in range(3)]
        if e == 5:
            return [spread_row(from_high[0, 8, c : c + 1, :]) for c in range(3)]
        return [spread_row(coefficients[c, 0, e - 1 : e, :]) for c in range(3)]

    return gains


def column_of(n):
    return 31 if n == 28 else 8 * (n // 7) + n % 7


def ghost_keep(message, i):
    return jnp.where(row_ids() == 7, message[i, 8], 1.0)


def finish_residual(image, source_part, outflow, from_low, from_high, low, middle, high):
    top = top_flags()
    for i in range(8):
        target, at = (low, i) if i < 2 else (middle, i - 2) if i < 6 else (high, i - 6)
        for y in range(31):
            if y == 0:
                keep = ghost_keep(from_low, i)
            elif y == 30:
                keep = ghost_keep(from_high, i)
            else:
                keep = own_keep(outflow, top, i, column_of(y - 1))
            target[at, y] = keep * (source_part[i, y] - image[i, y])


def first_body(
    dom, start, source, coefficients, outflow, from_low, from_high, own_table, side_table,
    plane_weights, field, source_part, low, middle, high, planes, image,
):
    lane = lane_ids()
    row = row_ids()
    inner_face = ((row == 0) & (lane > 0)) | ((row == 7) & (lane < 127))
    third_share = jnp.where(inner_face, 0.5, 1.0)
    place = dom[0]
    for i in range(8):
        if i == 0:
            share = third_share * jnp.where(place > 0, 0.5, 1.0)
        elif i == 7:
            share = third_share * jnp.where(place < dom[1] - 1, 0.5, 1.0)
        else:
            share = third_share
        field[i, 0:7] = from_low[i, 0:7]
        field[i, 36:43] = from_high[i, 0:7]
        source_part[i, 0] = from_low[i, 7] * share
        source_part[i, 30] = from_high[i, 7] * share
        for e in range(4):
            size = 8 if e == 3 else 7
            field[i, 7 + 7 * e : 7 + 7 * e + size] = start[i, 8 * e : 8 * e + size]
            source_part[i, 1 + 7 * e : 1 + 7 * e + size] = (
                source[i, 8 * e : 8 * e + size] * share[None]
            )
    residual_part(
        field, gains_of(coefficients, from_low, from_high), own_table, side_table,
        plane_weights, planes, image,
    )
    finish_residual(image, source_part, outflow, from_low, from_high, low, middle, high)


def whole(memory=None):
    return pl.BlockSpec(memory_space=memory or pltpu.VMEM)


def layers(count, rows):
    return jax.ShapeDtypeStruct((count, rows, 8, 128), F32)


def call(body, outs, kinds, scratch, name, args, flops):
    bytes_accessed = sum(4 * math.prod(a.shape) for a in args) + sum(
        4 * math.prod(o.shape) for o in outs
    )
    return pl.pallas_call(
        body,
        out_shape=tuple(outs),
        in_specs=[whole(pltpu.SMEM) if kind == "s" else whole() for kind in kinds],
        out_specs=tuple(whole() for _ in outs),
        scratch_shapes=scratch,
        compiler_params=pltpu.CompilerParams(vmem_limit_bytes=VMEM_BYTES),
        cost_estimate=pl.CostEstimate(
            flops=flops, bytes_accessed=bytes_accessed, transcendentals=0
        ),
        name=name,
    )(*args)


def operator_scratch():
    return [pltpu.VMEM((8, 128, 256), F32), pltpu.VMEM((8, 31, 8, 128), F32)]


def second_body(
    coefficients, outflow, from_low, from_high, own_table, side_table, plane_weights,
    field, source_part, correction, low_news, high_news,
    next_field, low, middle, high, planes, image,
):
    top = top_flags()
    for i in range(8):
        for y in range(31):
            value = correction[i, y]
            if y < 3:
                value = value + low_news[i, 6 + y]
            if y >= 28:
                value = value + high_news[i, y - 28]
            if y == 0:
                keep = ghost_keep(from_low, i)
            elif y == 30:
                keep = ghost_keep(from_high, i)
            else:
                keep = own_keep(outflow, top, i, column_of(y - 1))
            next_field[i, 6 + y] = field[i, 6 + y] + keep * value
        next_field[i, 0:6] = field[i, 0:6] + low_news[i, 0:6]
        next_field[i, 37:43] = field[i, 37:43] + high_news[i, 3:9]
    residual_part(
        next_field, gains_of(coefficients, from_low, from_high), own_table, side_table,
        plane_weights, planes, image,
    )
    finish_residual(image, source_part, outflow, from_low, from_high, low, middle, high)


def solve_body(
    last, coefficients, forward_high, forward_low, backward, backward_low, second_values,
    third_values, low, middle, high, from_low, from_high, *rest,
):
    if last:
        out_low, out_middle, out_high, residual, extended, spectral, halves = rest
    else:
        out_low, out_middle, out_high, extended, spectral, halves = rest
    lane = lane_ids()
    row = row_ids()

    def source_rows(a, y):
        if a == 0:
            return from_low[0, y]
        if a == 1:
            return low[0, y] + from_low[1, y]
        if a == 2:
            return low[1, y]
        if a < 7:
            return middle[a - 3, y]
        if a == 7:
            return high[0, y]
        if a == 8:
            return high[1, y] + from_high[0, y]
        return from_high[1, y]

    for a in range(10):

        def step(y, carry, a=a):
            value = source_rows(a, y)
            before = jnp.where(lane == 0, 0.0, pltpu.roll(value, 1, 1))
            after = jnp.where(lane == 127, 0.0, pltpu.roll(value, 127, 1))
            extended[0, a, y] = value
            extended[1, a, y] = before
            extended[2, a, y] = after
            return carry

        lax.fori_loop(0, 31, step, 0, unroll=True)

    if last:
        for i in range(8):
            for n in range(29):
                value = extended[0, i + 1, n + 1]
                value = (
                    value
                    + jnp.where(row == 0, pltpu.roll(extended[1, i + 1, n + 1], 1, 0), 0.0)
                    + jnp.where(row == 7, pltpu.roll(extended[2, i + 1, n + 1], 7, 0), 0.0)
                )
                residual[i, column_of(n)] = value
                if n % 7 == 0 and 0 < n < 28:
                    residual[i, column_of(n) - 1] = value

    def forward_step(a, carry):
        for pair in range(2):
            values = jnp.concatenate(
                [
                    jnp.concatenate(
                        [extended[g, a, 7 * e : 7 * e + 10].reshape(80, 128) for g in range(3)],
                        axis=0,
                    )
                    for e in (2 * pair, 2 * pair + 1)
                ],
                axis=1,
            )
            top, bottom = split(values)
            spectral[a, pair] = (
                dot(forward_high[...], top)
                + dot(forward_high[...], bottom)
                + dot(forward_low[...], top)
            )
        return carry

    lax.fori_loop(0, 10, forward_step, 0)

    def middle_step(block, carry):
        at = pl.multiple_of(16 * block, 16)
        second = second_values[pl.ds(at, 16), :]
        third = third_values[pl.ds(at, 16), :]
        for e in range(4):
            lanes = slice(128 * (e % 2), 128 * (e % 2) + 128)
            gain = [
                jnp.broadcast_to(coefficients[c, 0, e : e + 1, :], (16, 128)) for c in range(3)
            ]
            rest_sum = gain[1] * second + gain[2] * third
            values = [spectral[a, e // 2, pl.ds(at, 16), lanes] for a in range(10)]
            sums = [values[a] + values[9 - a] for a in range(5)]
            gaps = [values[a] - values[9 - a] for a in range(5)]
            modes = []
            for p in range(10):
                sides = sums if PARITY[p] > 0 else gaps
                total = sides[0] * float(HALF_BASIS[0, p])
                for a in range(1, 5):
                    total = total + sides[a] * float(HALF_BASIS[a, p])
                modes.append(total / (rest_sum + gain[0] * float(EIGEN[p])))
            for a in range(5):
                even = odd = None
                for p in EVEN:
                    term = modes[p] * float(HALF_BASIS[a, p])
                    even = term if even is None else even + term
                for p in ODD:
                    term = modes[p] * float(HALF_BASIS[a, p])
                    odd = term if odd is None else odd + term
                for place, value in ((a, even + odd), (9 - a, even - odd)):
                    top, bottom = split(value)
                    halves[place, e // 2, pl.ds(at, 16), lanes] = top
                    halves[place, e // 2, pl.ds(112 + at, 16), lanes] = bottom
        return carry

    lax.fori_loop(0, 7, middle_step, 0)

    def back_step(a, store):
        tail = None
        for pair in range(2):
            result = dot(backward[...], halves[a, pair]) + dot(
                backward_low[...], halves[a, pair, 0:112]
            )
            for half in range(2):
                e = 2 * pair + half
                rows = []
                for b in range(10):
                    main = result[8 * b : 8 * b + 8, 128 * half : 128 * half + 128]
                    side = result[80 + 8 * b : 88 + 8 * b, 128 * half : 128 * half + 128]
                    moved = jnp.where(
                        row < 4,
                        jnp.where(lane == 0, 0.0, pltpu.roll(side, 1, 1)),
                        jnp.where(lane == 127, 0.0, pltpu.roll(side, 127, 1)),
                    )
                    rows.append(main + moved)
                if tail is not None:
                    for b in range(3):
                        rows[b] = rows[b] + tail[b]
                for b in range(7):
                    store(7 * e + b, rows[b])
                tail = rows[7:]
        for b in range(3):
            store(28 + b, tail[b])

    for first, count, target in ((0, 2, out_low), (2, 6, out_middle), (8, 2, out_high)):

        def step(a, carry, first=first, target=target):
            def store(y, value):
                target[a, y] = value

            back_step(a + first, store)
            return carry

        lax.fori_loop(0, count, step, 0)


def solve(parts, received, coefficients, last):
    outs = [layers(2, 31), layers(6, 31), layers(2, 31)]
    if last:
        outs.append(layers(8, 32))
    tables = [jnp.asarray(t) for t in TRANSFORMS]
    return call(
        functools.partial(solve_body, last),
        outs,
        "v" * 12,
        [
            pltpu.VMEM((3, 10, 31, 8, 128), F32),
            pltpu.VMEM((10, 2, 112, 256), F32),
            pltpu.VMEM((10, 2, 224, 256), BF16),
        ],
        "local_solve",
        (coefficients, *tables, *parts, *received),
        10**9,
    )


def fold_rows(i, y, low, middle, high, from_low, from_high):
    if i == 0:
        return low[1, y] + from_low[0, y]
    if i == 1:
        return middle[0, y] + from_low[1, y]
    if i < 6:
        return middle[i - 1, y]
    if i == 6:
        return middle[5, y] + from_high[0, y]
    return high[0, y] + from_high[1, y]


def fold_body(last, outflow, low, middle, high, from_low, from_high, total, to_low, to_high):
    top = top_flags()
    count = 2 if last else 9
    for i in range(8):
        for y in range(31):
            value = fold_rows(i, y, low, middle, high, from_low, from_high)
            total[i, y] = value
            keep = lambda: own_keep(outflow, top, i, column_of(y - 1))
            if y < count:
                to_low[i, y] = value if y < 3 else keep() * value
            if y >= 31 - count:
                to_high[i, y - 31 + count] = value if y >= 28 else keep() * value


def fold(parts, received, outflow, last):
    count = 2 if last else 9
    return call(
        functools.partial(fold_body, last),
        [layers(8, 31), layers(8, count), layers(8, count)],
        "s" + "v" * 5,
        [],
        "fold",
        (outflow, *parts, *received),
        10**6,
    )


def final_body(outflow, field, correction, low_news, high_news, result):
    top = top_flags()
    for i in range(8):
        for n in range(29):
            value = correction[i, n + 1]
            if n < 2:
                value = value + low_news[i, n]
            if n >= 27:
                value = value + high_news[i, n - 27]
            column = column_of(n)
            value = field[i, n + 7] + own_keep(outflow, top, i, column) * value
            result[i, column] = value
            if n % 7 == 0 and 0 < n < 28:
                result[i, column - 1] = value


def exchange(to_low, to_high, axis):
    count = lax.axis_size(axis)
    upward = [(i, i + 1) for i in range(count - 1)]
    downward = [(i + 1, i) for i in range(count - 1)]
    return lax.ppermute(to_high, axis, upward), lax.ppermute(to_low, axis, downward)


def shards(start, source, coefficients, outflow):
    tables = [jnp.asarray(t) for t in (OPERATOR_OWN, OPERATOR_SIDE, PLANE_WEIGHTS)]
    dom = jnp.stack([lax.axis_index("dom"), lax.axis_size("dom")]).astype(jnp.int32)
    from_low, from_high = exchange(*pack_first(start, source, coefficients, outflow), "inner")
    field, source_part, *parts = call(
        first_body,
        [layers(8, 43), layers(8, 31), layers(2, 31), layers(4, 31), layers(2, 31)],
        "svvvsvvvvv",
        operator_scratch(),
        "first_residual",
        (dom, start, source, coefficients, outflow, from_low, from_high, *tables),
        10**8,
    )
    parts = solve(parts, exchange(parts[0], parts[2], "dom"), coefficients, False)
    total, to_low, to_high = fold(parts, exchange(parts[0], parts[2], "dom"), outflow, False)
    news = exchange(to_low, to_high, "inner")
    field, *parts = call(
        second_body,
        [layers(8, 43), layers(2, 31), layers(4, 31), layers(2, 31)],
        "vsvvvvvvvvvv",
        operator_scratch(),
        "second_residual",
        (coefficients, outflow, from_low, from_high, *tables, field, source_part, total, *news),
        10**8,
    )
    *parts, residual = solve(parts, exchange(parts[0], parts[2], "dom"), coefficients, True)
    total, to_low, to_high = fold(parts, exchange(parts[0], parts[2], "dom"), outflow, True)
    news = exchange(to_low, to_high, "inner")
    (iterate,) = call(
        final_body,
        [layers(8, 32)],
        "svvvv",
        [],
        "final_field",
        (outflow, field, total, *news),
        10**6,
    )
    return iterate, residual


def solution(mesh):
    placed = (
        P("dom", "inner", None, None),
        P("dom", "inner", None, None),
        P(None, "dom", "inner", None),
        P("dom", "inner"),
    )
    return jax.shard_map(
        shards,
        mesh=mesh,
        in_specs=placed,
        out_specs=(P("dom", "inner", None, None), P("dom", "inner", None, None)),
        check_vma=False,
    )
```

profile of v0, /device:TPU:25, one launch (start us, length us, event | category | flops | bytes accessed | tf_op | source)
XLA Modules:
  0.0 129.4 jit_solution(5140003507111429267)
XLA Ops:
  0.7 2.2 %pack_first.1 = (f32[8,9,8,128]{3,2,1,0:T(8,128)}, f32[8,9,8,128]{3,2,1,0:T(8,128)}) custom-call(f32[8,32,8,128]{3,2,1,0:T(8,128)} %start.1, f32[8,32,8,128]{3,2,1,0:T(8,128)} %start.1, f32[8,32,8,128]{3,2,1,0:T(8,128)} %source.1, f32[8,32,8,128]{3,2,1,0:T(8,128)} %source.1, f32[3,1,4,128]{3,2,1,0:T(4,128)} %coefficients.9, s32[8,32]{1,0:T(8,128)} %outflow.11), custom_call_target="tpu_custom_call" | custom-call | tf_op jit(solution)/shard_map/pack_first/pallas_call | solution.py:208
  2.9 3.7 %collective-permute-start = (f32[8,9,8,128]{3,2,1,0:T(8,128)}, f32[8,9,8,128]{3,2,1,0:T(8,128)S(1)}, u32[]{:S(2)}, u32[]{:S(2)}) collective-permute-start(f32[8,9,8,128]{3,2,1,0:T(8,128)} %get-tuple-element.26), channel_id=1, source_target_pairs={{0,1},{1,2},{2,3},{3,4},{4,5},{5,6},{6,7},{8,9},{9,10},{10,11},{11... | collective-permute-start | bytes 884744 | tf_op jit(solution)/shard_map/ppermute | solution.py:641
  10.5 4.3 %collective-permute-done.1.from_high = f32[8,9,8,128]{3,2,1,0:T(8,128)S(1)} collective-permute-done((f32[8,9,8,128]{3,2,1,0:T(8,128)}, f32[8,9,8,128]{3,2,1,0:T(8,128)S(1)}, u32[]{:S(2)}, u32[]{:S(2)}) %collective-permute-start.1) | collective-permute-done | bytes 294944 | tf_op jit(solution)/shard_map/ppermute | solution.py:641
  14.9 6.5 %first_residual.1 = (f32[8,43,8,128]{3,2,1,0:T(8,128)}, f32[8,31,8,128]{3,2,1,0:T(8,128)S(1)}, f32[2,31,8,128]{3,2,1,0:T(8,128)S(1)}, f32[4,31,8,128]{3,2,1,0:T(8,128)S(1)}, f32[2,31,8,128]{3,2,1,0:T(8,128)S(1)}) custom-call(s32[2]{0:T(128)S(1)} %pad_add_fusion.dom, f32[8,32,8,128]{3,2,1,0:T(8,128)S(1)} %copy-done, f32[8,32,8,128]{3,2,1,0:T(8,128)S(1)} %copy-done.1, ...), custom_call_target="tpu_custom_call" | custom-call | flops 100000000 | bytes 6315016 | tf_op jit(solution)/shard_map/first_residual/pallas_call | solution.py:366
  21.4 5.8 %collective-permute-start.3 = (f32[2,31,8,128]{3,2,1,0:T(8,128)S(1)}, f32[2,31,8,128]{3,2,1,0:T(8,128)S(1)}, u32[]{:S(2)}, u32[]{:S(2)}) collective-permute-start(f32[2,31,8,128]{3,2,1,0:T(8,128)S(1)} %get-tuple-element.30.low), channel_id=1, source_target_pairs={{8,0},{16,8},{24,16},{32,24},{40,32},{48,40},{56,48},{64,56},{72,6... | collective-permute-start | bytes 761864 | tf_op jit(solution)/shard_map/ppermute | solution.py:641
  30.4 5.9 %collective-permute-done.2.from_low = f32[2,31,8,128]{3,2,1,0:T(8,128)S(1)} collective-permute-done((f32[2,31,8,128]{3,2,1,0:T(8,128)S(1)}, f32[2,31,8,128]{3,2,1,0:T(8,128)S(1)}, u32[]{:S(2)}, u32[]{:S(2)}) %collective-permute-start.2) | collective-permute-done | bytes 253984 | tf_op jit(solution)/shard_map/ppermute | solution.py:641
  36.4 9.5 %local_solve.2 = (f32[2,31,8,128]{3,2,1,0:T(8,128)S(1)}, f32[6,31,8,128]{3,2,1,0:T(8,128)S(1)}, f32[2,31,8,128]{3,2,1,0:T(8,128)S(1)}) custom-call(f32[3,1,4,128]{3,2,1,0:T(4,128)S(1)} %copy-done.6, bf16[112,240]{1,0:T(8,128)(2,1)S(1)} %copy-done.11, bf16[112,240]{1,0:T(8,128)(2,1)S(1)} %copy-done.10, bf16[160,224]{1,0:T(8,128)(2,1)S(1)} %copy-done.7, ...), custom_call_target="tpu_custom_call" | custom-call | flops 1000000000 | bytes 3344384 | tf_op jit(solution)/shard_map/local_solve/pallas_call | solution.py:366
  45.9 1.9 %collective-permute-start.5 = (f32[2,31,8,128]{3,2,1,0:T(8,128)S(1)}, f32[2,31,8,128]{3,2,1,0:T(8,128)S(1)}, u32[]{:S(2)}, u32[]{:S(2)}) collective-permute-start(f32[2,31,8,128]{3,2,1,0:T(8,128)S(1)} %get-tuple-element.33.low), channel_id=1, source_target_pairs={{8,0},{16,8},{24,16},{32,24},{40,32},{48,40},{56,48},{64,56},{72,6... | collective-permute-start | bytes 761864 | tf_op jit(solution)/shard_map/ppermute | solution.py:641
  47.8 3.4 %collective-permute-start.4 = (f32[2,31,8,128]{3,2,1,0:T(8,128)S(1)}, f32[2,31,8,128]{3,2,1,0:T(8,128)S(1)}, u32[]{:S(2)}, u32[]{:S(2)}) collective-permute-start(f32[2,31,8,128]{3,2,1,0:T(8,128)S(1)} %get-tuple-element.35.high), channel_id=1, source_target_pairs={{0,8},{8,16},{16,24},{24,32},{32,40},{40,48},{48,56},{56,64},{64,7... | collective-permute-start | bytes 761864 | tf_op jit(solution)/shard_map/ppermute | solution.py:641
  51.2 2.1 %collective-permute-done.5.from_high = f32[2,31,8,128]{3,2,1,0:T(8,128)S(1)} collective-permute-done((f32[2,31,8,128]{3,2,1,0:T(8,128)S(1)}, f32[2,31,8,128]{3,2,1,0:T(8,128)S(1)}, u32[]{:S(2)}, u32[]{:S(2)}) %collective-permute-start.5) | collective-permute-done | bytes 253984 | tf_op jit(solution)/shard_map/ppermute | solution.py:641
  53.3 3.7 %collective-permute-done.4.from_low = f32[2,31,8,128]{3,2,1,0:T(8,128)S(1)} collective-permute-done((f32[2,31,8,128]{3,2,1,0:T(8,128)S(1)}, f32[2,31,8,128]{3,2,1,0:T(8,128)S(1)}, u32[]{:S(2)}, u32[]{:S(2)}) %collective-permute-start.4) | collective-permute-done | bytes 253984 | tf_op jit(solution)/shard_map/ppermute | solution.py:641
  57.7 8.7 %collective-permute-start.6 = (f32[8,9,8,128]{3,2,1,0:T(8,128)S(1)}, f32[8,9,8,128]{3,2,1,0:T(8,128)S(1)}, u32[]{:S(2)}, u32[]{:S(2)}) collective-permute-start(f32[8,9,8,128]{3,2,1,0:T(8,128)S(1)} %get-tuple-element.37), channel_id=1, source_target_pairs={{0,1},{1,2},{2,3},{3,4},{4,5},{5,6},{6,7},{8,9},{9,10},{10,11},{11... | collective-permute-start | bytes 884744 | tf_op jit(solution)/shard_map/ppermute | solution.py:641
  70.1 4.4 %collective-permute-done.7.high_news = f32[8,9,8,128]{3,2,1,0:T(8,128)S(1)} collective-permute-done((f32[8,9,8,128]{3,2,1,0:T(8,128)S(1)}, f32[8,9,8,128]{3,2,1,0:T(8,128)S(1)}, u32[]{:S(2)}, u32[]{:S(2)}) %collective-permute-start.7) | collective-permute-done | bytes 294944 | tf_op jit(solution)/shard_map/ppermute | solution.py:641
  74.4 6.3 %second_residual.1 = (f32[8,43,8,128]{3,2,1,0:T(8,128)S(1)}, f32[2,31,8,128]{3,2,1,0:T(8,128)S(1)}, f32[4,31,8,128]{3,2,1,0:T(8,128)S(1)}, f32[2,31,8,128]{3,2,1,0:T(8,128)S(1)}) custom-call(f32[3,1,4,128]{3,2,1,0:T(4,128)S(1)} %copy-done.6, s32[8,32]{1,0:T(8,128)S(1)} %copy-done.3, f32[8,9,8,128]{3,2,1,0:T(8,128)S(1)} %collective-permute-done.from_low, ...), custom_call_target="tpu_custom_call" | custom-call | flops 100000000 | bytes 7232512 | tf_op jit(solution)/shard_map/second_residual/pallas_call | solution.py:366
  82.7 3.4 %collective-permute-start.8 = (f32[2,31,8,128]{3,2,1,0:T(8,128)S(1)}, f32[2,31,8,128]{3,2,1,0:T(8,128)S(1)}, u32[]{:S(2)}, u32[]{:S(2)}) collective-permute-start(f32[2,31,8,128]{3,2,1,0:T(8,128)S(1)} %get-tuple-element.42.high), channel_id=1, source_target_pairs={{0,8},{8,16},{16,24},{24,32},{32,40},{40,48},{48,56},{56,64},{64,7... | collective-permute-start | bytes 761864 | tf_op jit(solution)/shard_map/ppermute | solution.py:641
  86.1 2.0 %collective-permute-done.9.from_high = f32[2,31,8,128]{3,2,1,0:T(8,128)S(1)} collective-permute-done((f32[2,31,8,128]{3,2,1,0:T(8,128)S(1)}, f32[2,31,8,128]{3,2,1,0:T(8,128)S(1)}, u32[]{:S(2)}, u32[]{:S(2)}) %collective-permute-start.9) | collective-permute-done | bytes 253984 | tf_op jit(solution)/shard_map/ppermute | solution.py:641
  88.0 3.8 %collective-permute-done.8.from_low = f32[2,31,8,128]{3,2,1,0:T(8,128)S(1)} collective-permute-done((f32[2,31,8,128]{3,2,1,0:T(8,128)S(1)}, f32[2,31,8,128]{3,2,1,0:T(8,128)S(1)}, u32[]{:S(2)}, u32[]{:S(2)}) %collective-permute-start.8) | collective-permute-done | bytes 253984 | tf_op jit(solution)/shard_map/ppermute | solution.py:641
  91.8 10.1 %local_solve.3 = (f32[2,31,8,128]{3,2,1,0:T(8,128)S(1)}, f32[6,31,8,128]{3,2,1,0:T(8,128)S(1)}, f32[2,31,8,128]{3,2,1,0:T(8,128)S(1)}, f32[8,32,8,128]{3,2,1,0:T(8,128)}) custom-call(f32[3,1,4,128]{3,2,1,0:T(4,128)S(1)} %copy-done.6, bf16[112,240]{1,0:T(8,128)(2,1)S(1)} %copy-done.11, bf16[112,240]{1,0:T(8,128)(2,1)S(1)} %copy-done.10, ...), custom_call_target="tpu_custom_call" | custom-call | flops 1000000000 | bytes 4392960 | tf_op jit(solution)/shard_map/local_solve/pallas_call | solution.py:366
  103.9 3.4 %collective-permute-start.10 = (f32[2,31,8,128]{3,2,1,0:T(8,128)S(1)}, f32[2,31,8,128]{3,2,1,0:T(8,128)S(1)}, u32[]{:S(2)}, u32[]{:S(2)}) collective-permute-start(f32[2,31,8,128]{3,2,1,0:T(8,128)S(1)} %get-tuple-element.45.high), channel_id=1, source_target_pairs={{0,8},{8,16},{16,24},{24,32},{32,40},{40,48},{48,56},{56,64},{64,7... | collective-permute-start | bytes 761864 | tf_op jit(solution)/shard_map/ppermute | solution.py:641
  107.3 2.0 %collective-permute-done.11.from_high = f32[2,31,8,128]{3,2,1,0:T(8,128)S(1)} collective-permute-done((f32[2,31,8,128]{3,2,1,0:T(8,128)S(1)}, f32[2,31,8,128]{3,2,1,0:T(8,128)S(1)}, u32[]{:S(2)}, u32[]{:S(2)}) %collective-permute-start.11) | collective-permute-done | bytes 253984 | tf_op jit(solution)/shard_map/ppermute | solution.py:641
  109.3 3.7 %collective-permute-done.10.from_low = f32[2,31,8,128]{3,2,1,0:T(8,128)S(1)} collective-permute-done((f32[2,31,8,128]{3,2,1,0:T(8,128)S(1)}, f32[2,31,8,128]{3,2,1,0:T(8,128)S(1)}, u32[]{:S(2)}, u32[]{:S(2)}) %collective-permute-start.10) | collective-permute-done | bytes 253984 | tf_op jit(solution)/shard_map/ppermute | solution.py:641
  113.7 8.3 %collective-permute-start.12 = (f32[8,2,8,128]{3,2,1,0:T(8,128)S(1)}, f32[8,2,8,128]{3,2,1,0:T(8,128)S(1)}, u32[]{:S(2)}, u32[]{:S(2)}) collective-permute-start(f32[8,2,8,128]{3,2,1,0:T(8,128)S(1)} %get-tuple-element.47), channel_id=1, source_target_pairs={{0,1},{1,2},{2,3},{3,4},{4,5},{5,6},{6,7},{8,9},{9,10},{10,11},{11... | collective-permute-start | bytes 196616 | tf_op jit(solution)/shard_map/ppermute | solution.py:641
  122.1 1.9 %collective-permute-start.13 = (f32[8,2,8,128]{3,2,1,0:T(8,128)S(1)}, f32[8,2,8,128]{3,2,1,0:T(8,128)S(1)}, u32[]{:S(2)}, u32[]{:S(2)}) collective-permute-start(f32[8,2,8,128]{3,2,1,0:T(8,128)S(1)} %get-tuple-element.48), channel_id=1, source_target_pairs={{1,0},{2,1},{3,2},{4,3},{5,4},{6,5},{7,6},{9,8},{10,9},{11,10},{12... | collective-permute-start | bytes 196616 | tf_op jit(solution)/shard_map/ppermute | solution.py:641
  124.0 3.6 %collective-permute-done.13.high_news = f32[8,2,8,128]{3,2,1,0:T(8,128)S(1)} collective-permute-done((f32[8,2,8,128]{3,2,1,0:T(8,128)S(1)}, f32[8,2,8,128]{3,2,1,0:T(8,128)S(1)}, u32[]{:S(2)}, u32[]{:S(2)}) %collective-permute-start.13) | collective-permute-done | bytes 65568 | tf_op jit(solution)/shard_map/ppermute | solution.py:641
  (39 shorter events, 17.8 us)
Async XLA Ops:
  0.6 14.2 %copy-start.2 = (bf16[128,192]{1,0:T(8,128)(2,1)S(1)}, bf16[128,192]{1,0:T(8,128)(2,1)}, u32[]{:S(2)}) copy-start(bf16[128,192]{1,0:T(8,128)(2,1)} %constant.26.clone.own_table) | copy-start | bytes 147460
  0.6 14.2 %copy-start.4 = (f32[8,8,128]{2,1,0:T(8,128)S(1)}, f32[8,8,128]{2,1,0:T(8,128)}, u32[]{:S(2)}) copy-start(f32[8,8,128]{2,1,0:T(8,128)} %constant.28.clone.plane_weights) | copy-start | bytes 98308
  0.7 14.2 %copy-start.5 = (bf16[64,192]{1,0:T(8,128)(2,1)S(1)}, bf16[64,192]{1,0:T(8,128)(2,1)}, u32[]{:S(2)}) copy-start(bf16[64,192]{1,0:T(8,128)(2,1)} %constant.27.clone.side_table) | copy-start | bytes 73732
  0.7 14.2 %copy-start.3 = (s32[8,32]{1,0:T(8,128)S(1)}, s32[8,32]{1,0:T(8,128)}, u32[]{:S(2)}) copy-start(s32[8,32]{1,0:T(8,128)} %outflow.11) | copy-start | bytes 3076
  2.9 7.6 %collective-permute-start = (f32[8,9,8,128]{3,2,1,0:T(8,128)}, f32[8,9,8,128]{3,2,1,0:T(8,128)S(1)}, u32[]{:S(2)}, u32[]{:S(2)}) collective-permute-start(f32[8,9,8,128]{3,2,1,0:T(8,128)} %get-tuple-element.26), channel_id=1, source_target_pairs={{0,1},{1,2},{2,3},{3,4},{4,5},{5,6},{6,7},{8,9},{9,10},{10,11},{11... | collective-permute-start | bytes 884744 | tf_op jit(solution)/shard_map/ppermute | solution.py:641
  6.6 8.3 %collective-permute-start.1 = (f32[8,9,8,128]{3,2,1,0:T(8,128)}, f32[8,9,8,128]{3,2,1,0:T(8,128)S(1)}, u32[]{:S(2)}, u32[]{:S(2)}) collective-permute-start(f32[8,9,8,128]{3,2,1,0:T(8,128)} %get-tuple-element.27), channel_id=1, source_target_pairs={{1,0},{2,1},{3,2},{4,3},{5,4},{6,5},{7,6},{9,8},{10,9},{11,10},{12... | collective-permute-start | bytes 884744 | tf_op jit(solution)/shard_map/ppermute | solution.py:641
  8.6 27.8 %copy-start.7 = (bf16[160,224]{1,0:T(8,128)(2,1)S(1)}, bf16[160,224]{1,0:T(8,128)(2,1)}, u32[]{:S(2)}) copy-start(bf16[160,224]{1,0:T(8,128)(2,1)} %constant.31.clone.backward) | copy-start | bytes 215044
  8.6 27.8 %copy-start.8 = (f32[112,128]{1,0:T(8,128)S(1)}, f32[112,128]{1,0:T(8,128)}, u32[]{:S(2)}) copy-start(f32[112,128]{1,0:T(8,128)} %constant.34.clone.third_values) | copy-start | bytes 172036
  8.6 27.8 %copy-start.9 = (f32[112,128]{1,0:T(8,128)S(1)}, f32[112,128]{1,0:T(8,128)}, u32[]{:S(2)}) copy-start(f32[112,128]{1,0:T(8,128)} %constant.33.clone.second_values) | copy-start | bytes 172036
  8.6 27.8 %copy-start.10 = (bf16[112,240]{1,0:T(8,128)(2,1)S(1)}, bf16[112,240]{1,0:T(8,128)(2,1)}, u32[]{:S(2)}) copy-start(bf16[112,240]{1,0:T(8,128)(2,1)} %constant.30.clone.forward_low) | copy-start | bytes 161284
  8.6 27.8 %copy-start.11 = (bf16[112,240]{1,0:T(8,128)(2,1)S(1)}, bf16[112,240]{1,0:T(8,128)(2,1)}, u32[]{:S(2)}) copy-start(bf16[112,240]{1,0:T(8,128)(2,1)} %constant.29.clone.forward_high) | copy-start | bytes 161284
  8.6 27.8 %copy-start.12 = (bf16[160,112]{1,0:T(8,128)(2,1)S(1)}, bf16[160,112]{1,0:T(8,128)(2,1)}, u32[]{:S(2)}) copy-start(bf16[160,112]{1,0:T(8,128)(2,1)} %constant.32.clone.backward_low) | copy-start | bytes 107524
  21.4 9.1 %collective-permute-start.3 = (f32[2,31,8,128]{3,2,1,0:T(8,128)S(1)}, f32[2,31,8,128]{3,2,1,0:T(8,128)S(1)}, u32[]{:S(2)}, u32[]{:S(2)}) collective-permute-start(f32[2,31,8,128]{3,2,1,0:T(8,128)S(1)} %get-tuple-element.30.low), channel_id=1, source_target_pairs={{8,0},{16,8},{24,16},{32,24},{40,32},{48,40},{56,48},{64,56},{72,6... | collective-permute-start | bytes 761864 | tf_op jit(solution)/shard_map/ppermute | solution.py:641
  27.2 9.1 %collective-permute-start.2 = (f32[2,31,8,128]{3,2,1,0:T(8,128)S(1)}, f32[2,31,8,128]{3,2,1,0:T(8,128)S(1)}, u32[]{:S(2)}, u32[]{:S(2)}) collective-permute-start(f32[2,31,8,128]{3,2,1,0:T(8,128)S(1)} %get-tuple-element.32.high), channel_id=1, source_target_pairs={{0,8},{8,16},{16,24},{24,32},{32,40},{40,48},{48,56},{56,64},{64,7... | collective-permute-start | bytes 761864 | tf_op jit(solution)/shard_map/ppermute | solution.py:641
  45.9 7.4 %collective-permute-start.5 = (f32[2,31,8,128]{3,2,1,0:T(8,128)S(1)}, f32[2,31,8,128]{3,2,1,0:T(8,128)S(1)}, u32[]{:S(2)}, u32[]{:S(2)}) collective-permute-start(f32[2,31,8,128]{3,2,1,0:T(8,128)S(1)} %get-tuple-element.33.low), channel_id=1, source_target_pairs={{8,0},{16,8},{24,16},{32,24},{40,32},{48,40},{56,48},{64,56},{72,6... | collective-permute-start | bytes 761864 | tf_op jit(solution)/shard_map/ppermute | solution.py:641
  47.8 9.2 %collective-permute-start.4 = (f32[2,31,8,128]{3,2,1,0:T(8,128)S(1)}, f32[2,31,8,128]{3,2,1,0:T(8,128)S(1)}, u32[]{:S(2)}, u32[]{:S(2)}) collective-permute-start(f32[2,31,8,128]{3,2,1,0:T(8,128)S(1)} %get-tuple-element.35.high), channel_id=1, source_target_pairs={{0,8},{8,16},{16,24},{24,32},{32,40},{40,48},{48,56},{56,64},{64,7... | collective-permute-start | bytes 761864 | tf_op jit(solution)/shard_map/ppermute | solution.py:641
  57.7 12.3 %collective-permute-start.6 = (f32[8,9,8,128]{3,2,1,0:T(8,128)S(1)}, f32[8,9,8,128]{3,2,1,0:T(8,128)S(1)}, u32[]{:S(2)}, u32[]{:S(2)}) collective-permute-start(f32[8,9,8,128]{3,2,1,0:T(8,128)S(1)} %get-tuple-element.37), channel_id=1, source_target_pairs={{0,1},{1,2},{2,3},{3,4},{4,5},{5,6},{6,7},{8,9},{9,10},{10,11},{11... | collective-permute-start | bytes 884744 | tf_op jit(solution)/shard_map/ppermute | solution.py:641
  66.4 8.0 %collective-permute-start.7 = (f32[8,9,8,128]{3,2,1,0:T(8,128)S(1)}, f32[8,9,8,128]{3,2,1,0:T(8,128)S(1)}, u32[]{:S(2)}, u32[]{:S(2)}) collective-permute-start(f32[8,9,8,128]{3,2,1,0:T(8,128)S(1)} %get-tuple-element.38), channel_id=1, source_target_pairs={{1,0},{2,1},{3,2},{4,3},{5,4},{6,5},{7,6},{9,8},{10,9},{11,10},{12... | collective-permute-start | bytes 884744 | tf_op jit(solution)/shard_map/ppermute | solution.py:641
  80.8 7.3 %collective-permute-start.9 = (f32[2,31,8,128]{3,2,1,0:T(8,128)S(1)}, f32[2,31,8,128]{3,2,1,0:T(8,128)S(1)}, u32[]{:S(2)}, u32[]{:S(2)}) collective-permute-start(f32[2,31,8,128]{3,2,1,0:T(8,128)S(1)} %get-tuple-element.40.low), channel_id=1, source_target_pairs={{8,0},{16,8},{24,16},{32,24},{40,32},{48,40},{56,48},{64,56},{72,6... | collective-permute-start | bytes 761864 | tf_op jit(solution)/shard_map/ppermute | solution.py:641
  82.7 9.1 %collective-permute-start.8 = (f32[2,31,8,128]{3,2,1,0:T(8,128)S(1)}, f32[2,31,8,128]{3,2,1,0:T(8,128)S(1)}, u32[]{:S(2)}, u32[]{:S(2)}) collective-permute-start(f32[2,31,8,128]{3,2,1,0:T(8,128)S(1)} %get-tuple-element.42.high), channel_id=1, source_target_pairs={{0,8},{8,16},{16,24},{24,32},{32,40},{40,48},{48,56},{56,64},{64,7... | collective-permute-start | bytes 761864 | tf_op jit(solution)/shard_map/ppermute | solution.py:641
  102.0 7.3 %collective-permute-start.11 = (f32[2,31,8,128]{3,2,1,0:T(8,128)S(1)}, f32[2,31,8,128]{3,2,1,0:T(8,128)S(1)}, u32[]{:S(2)}, u32[]{:S(2)}) collective-permute-start(f32[2,31,8,128]{3,2,1,0:T(8,128)S(1)} %get-tuple-element.43.low), channel_id=1, source_target_pairs={{8,0},{16,8},{24,16},{32,24},{40,32},{48,40},{56,48},{64,56},{72,6... | collective-permute-start | bytes 761864 | tf_op jit(solution)/shard_map/ppermute | solution.py:641
  103.9 9.1 %collective-permute-start.10 = (f32[2,31,8,128]{3,2,1,0:T(8,128)S(1)}, f32[2,31,8,128]{3,2,1,0:T(8,128)S(1)}, u32[]{:S(2)}, u32[]{:S(2)}) collective-permute-start(f32[2,31,8,128]{3,2,1,0:T(8,128)S(1)} %get-tuple-element.45.high), channel_id=1, source_target_pairs={{0,8},{8,16},{16,24},{24,32},{32,40},{40,48},{48,56},{56,64},{64,7... | collective-permute-start | bytes 761864 | tf_op jit(solution)/shard_map/ppermute | solution.py:641
  113.7 10.3 %collective-permute-start.12 = (f32[8,2,8,128]{3,2,1,0:T(8,128)S(1)}, f32[8,2,8,128]{3,2,1,0:T(8,128)S(1)}, u32[]{:S(2)}, u32[]{:S(2)}) collective-permute-start(f32[8,2,8,128]{3,2,1,0:T(8,128)S(1)} %get-tuple-element.47), channel_id=1, source_target_pairs={{0,1},{1,2},{2,3},{3,4},{4,5},{5,6},{6,7},{8,9},{9,10},{10,11},{11... | collective-permute-start | bytes 196616 | tf_op jit(solution)/shard_map/ppermute | solution.py:641
  122.1 5.6 %collective-permute-start.13 = (f32[8,2,8,128]{3,2,1,0:T(8,128)S(1)}, f32[8,2,8,128]{3,2,1,0:T(8,128)S(1)}, u32[]{:S(2)}, u32[]{:S(2)}) collective-permute-start(f32[8,2,8,128]{3,2,1,0:T(8,128)S(1)} %get-tuple-element.48), channel_id=1, source_target_pairs={{1,0},{2,1},{3,2},{4,3},{5,4},{6,5},{7,6},{9,8},{10,9},{11,10},{12... | collective-permute-start | bytes 196616 | tf_op jit(solution)/shard_map/ppermute | solution.py:641
  (3 other events, 42.5 us)
where the time goes:
time: 130 us; the launch traced here: 129 us
  starting transfers between devices  50 us (38%)
  waiting for transfers between devices  40.5 us (31%)
  Pallas kernels  37.8 us (29%)
    pallas_call x7, Pallas kernels, call(): pl.pallas_call(body, out_shape=tuple(outs), in_specs=[whole(pltpu.SMEM) i...  35.6 us
    ppermute x7, starting transfers between devices, exchange(): lax.ppermute(to_high, axis, upward)  32.7 us
    ppermute x7, waiting for transfers between devices, exchange(): lax.ppermute(to_high, axis, upward)  20.9 us
    ppermute x7, waiting for transfers between devices, exchange(): lax.ppermute(to_low, axis, downward)  19.7 us
    ppermute x7, starting transfers between devices, exchange(): lax.ppermute(to_low, axis, downward)  17.4 us
  transfers between devices with their start and end apart: 14, of which 13 were waited for; matrix products, arithmetic and copies ran while one was open for 0% of the time, Pallas kernels for 0%

commit v1 on v0

--- a/solution.py
+++ b/solution.py
@@ -173,6 +173,13 @@
     return jnp.dot(left, right, preferred_element_type=F32)
 
 
+def ends(place, axis):
+    return (
+        jnp.where(place[2 * axis] > 0, 1.0, 0.0),
+        jnp.where(place[2 * axis] < place[2 * axis + 1] - 1, 1.0, 0.0),
+    )
+
+
 def top_flags():
     return ((lane_ids() == 127) & (row_ids() == 7)).astype(F32)
 
@@ -285,12 +292,14 @@
             combine(e, lane, 7, 56, 120, base + 7, e == 4)
 
 
-def gains_of(coefficients, from_low, from_high):
+def gains_of(place, coefficients, from_low, from_high):
+    low_flag, high_flag = ends(place, 1)
+
     def gains(e):
         if e == 0:
-            return [spread_row(from_low[0, 8, c : c + 1, :]) for c in range(3)]
+            return [spread_row(from_low[0, 8, c : c + 1, :] * low_flag) for c in range(3)]
         if e == 5:
-            return [spread_row(from_high[0, 8, c : c + 1, :]) for c in range(3)]
+            return [spread_row(from_high[0, 8, c : c + 1, :] * high_flag) for c in range(3)]
         return [spread_row(coefficients[c, 0, e - 1 : e, :]) for c in range(3)]
 
     return gains
@@ -319,25 +328,26 @@
 
 
 def first_body(
-    dom, start, source, coefficients, outflow, from_low, from_high, own_table, side_table,
+    place, start, source, coefficients, outflow, from_low, from_high, own_table, side_table,
     plane_weights, field, source_part, low, middle, high, planes, image,
 ):
     lane = lane_ids()
     row = row_ids()
     inner_face = ((row == 0) & (lane > 0)) | ((row == 7) & (lane < 127))
     third_share = jnp.where(inner_face, 0.5, 1.0)
-    place = dom[0]
+    below, above = ends(place, 0)
+    low_flag, high_flag = ends(place, 1)
     for i in range(8):
         if i == 0:
-            share = third_share * jnp.where(place > 0, 0.5, 1.0)
+            share = third_share * (1.0 - 0.5 * below)
         elif i == 7:
-            share = third_share * jnp.where(place < dom[1] - 1, 0.5, 1.0)
+            share = third_share * (1.0 - 0.5 * above)
         else:
             share = third_share
         field[i, 0:7] = from_low[i, 0:7]
         field[i, 36:43] = from_high[i, 0:7]
-        source_part[i, 0] = from_low[i, 7] * share
-        source_part[i, 30] = from_high[i, 7] * share
+        source_part[i, 0] = from_low[i, 7] * (share * low_flag)
+        source_part[i, 30] = from_high[i, 7] * (share * high_flag)
         for e in range(4):
             size = 8 if e == 3 else 7
             field[i, 7 + 7 * e : 7 + 7 * e + size] = start[i, 8 * e : 8 * e + size]
@@ -345,7 +355,7 @@
                 source[i, 8 * e : 8 * e + size] * share[None]
             )
     residual_part(
-        field, gains_of(coefficients, from_low, from_high), own_table, side_table,
+        field, gains_of(place, coefficients, from_low, from_high), own_table, side_table,
         plane_weights, planes, image,
     )
     finish_residual(image, source_part, outflow, from_low, from_high, low, middle, high)
@@ -382,18 +392,19 @@
 
 
 def second_body(
-    coefficients, outflow, from_low, from_high, own_table, side_table, plane_weights,
+    place, coefficients, outflow, from_low, from_high, own_table, side_table, plane_weights,
     field, source_part, correction, low_news, high_news,
     next_field, low, middle, high, planes, image,
 ):
     top = top_flags()
+    low_flag, high_flag = ends(place, 1)
     for i in range(8):
         for y in range(31):
             value = correction[i, y]
             if y < 3:
-                value = value + low_news[i, 6 + y]
+                value = value + low_flag * low_news[i, 6 + y]
             if y >= 28:
-                value = value + high_news[i, y - 28]
+                value = value + high_flag * high_news[i, y - 28]
             if y == 0:
                 keep = ghost_keep(from_low, i)
             elif y == 30:
@@ -404,14 +415,14 @@
         next_field[i, 0:6] = field[i, 0:6] + low_news[i, 0:6]
         next_field[i, 37:43] = field[i, 37:43] + high_news[i, 3:9]
     residual_part(
-        next_field, gains_of(coefficients, from_low, from_high), own_table, side_table,
+        next_field, gains_of(place, coefficients, from_low, from_high), own_table, side_table,
         plane_weights, planes, image,
     )
     finish_residual(image, source_part, outflow, from_low, from_high, low, middle, high)
 
 
 def solve_body(
-    last, coefficients, forward_high, forward_low, backward, backward_low, second_values,
+    last, place, coefficients, forward_high, forward_low, backward, backward_low, second_values,
     third_values, low, middle, high, from_low, from_high, *rest,
 ):
     if last:
@@ -420,12 +431,13 @@
         out_low, out_middle, out_high, extended, spectral, halves = rest
     lane = lane_ids()
     row = row_ids()
+    below, above = ends(place, 0)
 
     def source_rows(a, y):
         if a == 0:
-            return from_low[0, y]
+            return below * from_low[0, y]
         if a == 1:
-            return low[0, y] + from_low[1, y]
+            return low[0, y] + below * from_low[1, y]
         if a == 2:
             return low[1, y]
         if a < 7:
@@ -433,8 +445,8 @@
         if a == 7:
             return high[0, y]
         if a == 8:
-            return high[1, y] + from_high[0, y]
-        return from_high[1, y]
+            return high[1, y] + above * from_high[0, y]
+        return above * from_high[1, y]
 
     for a in range(10):
 
@@ -559,7 +571,7 @@
         lax.fori_loop(0, count, step, 0)
 
 
-def solve(parts, received, coefficients, last):
+def solve(place, parts, received, coefficients, last):
     outs = [layers(2, 31), layers(6, 31), layers(2, 31)]
     if last:
         outs.append(layers(8, 32))
@@ -567,36 +579,37 @@
     return call(
         functools.partial(solve_body, last),
         outs,
-        "v" * 12,
+        "s" + "v" * 12,
         [
             pltpu.VMEM((3, 10, 31, 8, 128), F32),
             pltpu.VMEM((10, 2, 112, 256), F32),
             pltpu.VMEM((10, 2, 224, 256), BF16),
         ],
         "local_solve",
-        (coefficients, *tables, *parts, *received),
+        (place, coefficients, *tables, *parts, *received),
         10**9,
     )
 
 
-def fold_rows(i, y, low, middle, high, from_low, from_high):
+def fold_rows(place, i, y, low, middle, high, from_low, from_high):
+    below, above = ends(place, 0)
     if i == 0:
-        return low[1, y] + from_low[0, y]
+        return low[1, y] + below * from_low[0, y]
     if i == 1:
-        return middle[0, y] + from_low[1, y]
+        return middle[0, y] + below * from_low[1, y]
     if i < 6:
         return middle[i - 1, y]
     if i == 6:
-        return middle[5, y] + from_high[0, y]
-    return high[0, y] + from_high[1, y]
-
-
-def fold_body(last, outflow, low, middle, high, from_low, from_high, total, to_low, to_high):
+        return middle[5, y] + above * from_high[0, y]
+    return high[0, y] + above * from_high[1, y]
+
+
+def fold_body(last, place, outflow, low, middle, high, from_low, from_high, total, to_low, to_high):
     top = top_flags()
     count = 2 if last else 9
     for i in range(8):
         for y in range(31):
-            value = fold_rows(i, y, low, middle, high, from_low, from_high)
+            value = fold_rows(place, i, y, low, middle, high, from_low, from_high)
             total[i, y] = value
             keep = lambda: own_keep(outflow, top, i, column_of(y - 1))
             if y < count:
@@ -605,28 +618,29 @@
                 to_high[i, y - 31 + count] = value if y >= 28 else keep() * value
 
 
-def fold(parts, received, outflow, last):
+def fold(place, parts, received, outflow, last):
     count = 2 if last else 9
     return call(
         functools.partial(fold_body, last),
         [layers(8, 31), layers(8, count), layers(8, count)],
-        "s" + "v" * 5,
+        "ss" + "v" * 5,
         [],
         "fold",
-        (outflow, *parts, *received),
+        (place, outflow, *parts, *received),
         10**6,
     )
 
 
-def final_body(outflow, field, correction, low_news, high_news, result):
+def final_body(place, outflow, field, correction, low_news, high_news, result):
     top = top_flags()
+    low_flag, high_flag = ends(place, 1)
     for i in range(8):
         for n in range(29):
             value = correction[i, n + 1]
             if n < 2:
-                value = value + low_news[i, n]
+                value = value + low_flag * low_news[i, n]
             if n >= 27:
-                value = value + high_news[i, n - 27]
+                value = value + high_flag * high_news[i, n - 27]
             column = column_of(n)
             value = field[i, n + 7] + own_keep(outflow, top, i, column) * value
             result[i, column] = value
@@ -636,14 +650,21 @@
 
 def exchange(to_low, to_high, axis):
     count = lax.axis_size(axis)
-    upward = [(i, i + 1) for i in range(count - 1)]
-    downward = [(i + 1, i) for i in range(count - 1)]
+    upward = [(i, (i + 1) % count) for i in range(count)]
+    downward = [((i + 1) % count, i) for i in range(count)]
     return lax.ppermute(to_high, axis, upward), lax.ppermute(to_low, axis, downward)
 
 
 def shards(start, source, coefficients, outflow):
     tables = [jnp.asarray(t) for t in (OPERATOR_OWN, OPERATOR_SIDE, PLANE_WEIGHTS)]
-    dom = jnp.stack([lax.axis_index("dom"), lax.axis_size("dom")]).astype(jnp.int32)
+    place = jnp.stack(
+        [
+            lax.axis_index("dom"),
+            lax.axis_size("dom"),
+            lax.axis_index("inner"),
+            lax.axis_size("inner"),
+        ]
+    ).astype(jnp.int32)
     from_low, from_high = exchange(*pack_first(start, source, coefficients, outflow), "inner")
     field, source_part, *parts = call(
         first_body,
@@ -651,31 +672,34 @@
         "svvvsvvvvv",
         operator_scratch(),
         "first_residual",
-        (dom, start, source, coefficients, outflow, from_low, from_high, *tables),
+        (place, start, source, coefficients, outflow, from_low, from_high, *tables),
         10**8,
     )
-    parts = solve(parts, exchange(parts[0], parts[2], "dom"), coefficients, False)
-    total, to_low, to_high = fold(parts, exchange(parts[0], parts[2], "dom"), outflow, False)
+    parts = solve(place, parts, exchange(parts[0], parts[2], "dom"), coefficients, False)
+    total, to_low, to_high = fold(place, parts, exchange(parts[0], parts[2], "dom"), outflow, False)
     news = exchange(to_low, to_high, "inner")
     field, *parts = call(
         second_body,
         [layers(8, 43), layers(2, 31), layers(4, 31), layers(2, 31)],
-        "vsvvvvvvvvvv",
+        "svsvvvvvvvvvv",
         operator_scratch(),
         "second_residual",
-        (coefficients, outflow, from_low, from_high, *tables, field, source_part, total, *news),
+        (
+            place, coefficients, outflow, from_low, from_high, *tables, field, source_part,
+            total, *news,
+        ),
         10**8,
     )
-    *parts, residual = solve(parts, exchange(parts[0], parts[2], "dom"), coefficients, True)
-    total, to_low, to_high = fold(parts, exchange(parts[0], parts[2], "dom"), outflow, True)
+    *parts, residual = solve(place, parts, exchange(parts[0], parts[2], "dom"), coefficients, True)
+    total, to_low, to_high = fold(place, parts, exchange(parts[0], parts[2], "dom"), outflow, True)
     news = exchange(to_low, to_high, "inner")
     (iterate,) = call(
         final_body,
         [layers(8, 32)],
-        "svvvv",
+        "ssvvvv",
         [],
         "final_field",
-        (outflow, field, total, *news),
+        (place, outflow, field, total, *news),
         10**6,
     )
     return iterate, residual

time: 130 us -> 113 us (0.87)
  the two profiles are of different devices: /device:TPU:25 before, /device:TPU:1 now
where the time goes in v1:
time: 113 us; the launch traced here: 112 us
  waiting for transfers between devices  53 us (47%)
  Pallas kernels  38.8 us (34%)
  starting transfers between devices  19.6 us (17%)
    pallas_call x7, Pallas kernels, call(): pl.pallas_call(body, out_shape=tuple(outs), in_specs=[whole(pltpu.SMEM) i...  36.6 us
    ppermute x7, waiting for transfers between devices, exchange(): lax.ppermute(to_low, axis, downward)  28.7 us
    ppermute x7, waiting for transfers between devices, exchange(): lax.ppermute(to_high, axis, upward)  24.3 us
    ppermute x7, starting transfers between devices, exchange(): lax.ppermute(to_high, axis, upward)  12.8 us
    ppermute x7, starting transfers between devices, exchange(): lax.ppermute(to_low, axis, downward)  6.84 us
  transfers between devices with their start and end apart: 14, of which 14 were waited for; matrix products, arithmetic and copies ran while one was open for 0% of the time, Pallas kernels for 0%

profile of v1, /device:TPU:1, one launch (start us, length us, event | category | flops | bytes accessed | tf_op | source)
XLA Modules:
  0.0 112.4 jit_solution(14970886531724319389)
XLA Ops:
  0.7 2.2 %pack_first.1 = (f32[8,9,8,128]{3,2,1,0:T(8,128)}, f32[8,9,8,128]{3,2,1,0:T(8,128)}) custom-call(f32[8,32,8,128]{3,2,1,0:T(8,128)} %start.1, f32[8,32,8,128]{3,2,1,0:T(8,128)} %start.1, f32[8,32,8,128]{3,2,1,0:T(8,128)} %source.1, f32[8,32,8,128]{3,2,1,0:T(8,128)} %source.1, f32[3,1,4,128]{3,2,1,0:T(4,128)} %coefficients.9, s32[8,32]{1,0:T(8,128)} %outflow.11), custom_call_target="tpu_custom_call" | custom-call | tf_op jit(solution)/shard_map/pack_first/pallas_call | solution.py:215
  2.9 2.6 %collective-permute-start = (f32[8,9,8,128]{3,2,1,0:T(8,128)}, f32[8,9,8,128]{3,2,1,0:T(8,128)S(1)}, u32[]{:S(2)}, u32[]{:S(2)}) collective-permute-start(f32[8,9,8,128]{3,2,1,0:T(8,128)} %get-tuple-element.26), channel_id=1, source_target_pairs={{0,1},{1,2},{2,3},{3,4},{4,5},{5,6},{6,7},{7,0},{8,9},{9,10},{10,1... | collective-permute-start | bytes 884744 | tf_op jit(solution)/shard_map/ppermute | solution.py:655
  5.6 3.9 %collective-permute-done.from_low = f32[8,9,8,128]{3,2,1,0:T(8,128)S(1)} collective-permute-done((f32[8,9,8,128]{3,2,1,0:T(8,128)}, f32[8,9,8,128]{3,2,1,0:T(8,128)S(1)}, u32[]{:S(2)}, u32[]{:S(2)}) %collective-permute-start) | collective-permute-done | bytes 294944 | tf_op jit(solution)/shard_map/ppermute | solution.py:655
  9.5 2.4 %collective-permute-done.1.from_high = f32[8,9,8,128]{3,2,1,0:T(8,128)S(1)} collective-permute-done((f32[8,9,8,128]{3,2,1,0:T(8,128)}, f32[8,9,8,128]{3,2,1,0:T(8,128)S(1)}, u32[]{:S(2)}, u32[]{:S(2)}) %collective-permute-start.1) | collective-permute-done | bytes 294944 | tf_op jit(solution)/shard_map/ppermute | solution.py:655
  11.9 6.4 %first_residual.1 = (f32[8,43,8,128]{3,2,1,0:T(8,128)}, f32[8,31,8,128]{3,2,1,0:T(8,128)S(1)}, f32[2,31,8,128]{3,2,1,0:T(8,128)S(1)}, f32[4,31,8,128]{3,2,1,0:T(8,128)S(1)}, f32[2,31,8,128]{3,2,1,0:T(8,128)S(1)}) custom-call(s32[4]{0:T(128)S(1)} %pad_add_fusion.place, f32[8,32,8,128]{3,2,1,0:T(8,128)S(1)} %copy-done, f32[8,32,8,128]{3,2,1,0:T(8,128)S(1)} %copy-done.1, ...), custom_call_target="tpu_custom_call" | custom-call | flops 100000000 | bytes 6315024 | tf_op jit(solution)/shard_map/first_residual/pallas_call | solution.py:376
  18.3 6.2 %collective-permute-start.3 = (f32[2,31,8,128]{3,2,1,0:T(8,128)S(1)}, f32[2,31,8,128]{3,2,1,0:T(8,128)S(1)}, u32[]{:S(2)}, u32[]{:S(2)}) collective-permute-start(f32[2,31,8,128]{3,2,1,0:T(8,128)S(1)} %get-tuple-element.30.low), channel_id=1, source_target_pairs={{8,0},{16,8},{24,16},{32,24},{40,32},{48,40},{56,48},{64,56},{72,6... | collective-permute-start | bytes 761864 | tf_op jit(solution)/shard_map/ppermute | solution.py:655
  24.6 5.4 %collective-permute-done.3.from_high = f32[2,31,8,128]{3,2,1,0:T(8,128)S(1)} collective-permute-done((f32[2,31,8,128]{3,2,1,0:T(8,128)S(1)}, f32[2,31,8,128]{3,2,1,0:T(8,128)S(1)}, u32[]{:S(2)}, u32[]{:S(2)}) %collective-permute-start.3) | collective-permute-done | bytes 253984 | tf_op jit(solution)/shard_map/ppermute | solution.py:655
  30.0 5.2 %collective-permute-done.2.from_low = f32[2,31,8,128]{3,2,1,0:T(8,128)S(1)} collective-permute-done((f32[2,31,8,128]{3,2,1,0:T(8,128)S(1)}, f32[2,31,8,128]{3,2,1,0:T(8,128)S(1)}, u32[]{:S(2)}, u32[]{:S(2)}) %collective-permute-start.2) | collective-permute-done | bytes 253984 | tf_op jit(solution)/shard_map/ppermute | solution.py:655
  35.2 10.1 %local_solve.2 = (f32[2,31,8,128]{3,2,1,0:T(8,128)S(1)}, f32[6,31,8,128]{3,2,1,0:T(8,128)S(1)}, f32[2,31,8,128]{3,2,1,0:T(8,128)S(1)}) custom-call(s32[4]{0:T(128)S(1)} %pad_add_fusion.place, f32[3,1,4,128]{3,2,1,0:T(4,128)S(1)} %copy-done.6, bf16[112,240]{1,0:T(8,128)(2,1)S(1)} %copy-done.11, bf16[112,240]{1,0:T(8,128)(2,1)S(1)} %copy-done.10, ...), custom_call_target="tpu_custom_call" | custom-call | flops 1000000000 | bytes 3344400 | tf_op jit(solution)/shard_map/local_solve/pallas_call | solution.py:376
  46.8 4.9 %collective-permute-done.5.from_high = f32[2,31,8,128]{3,2,1,0:T(8,128)S(1)} collective-permute-done((f32[2,31,8,128]{3,2,1,0:T(8,128)S(1)}, f32[2,31,8,128]{3,2,1,0:T(8,128)S(1)}, u32[]{:S(2)}, u32[]{:S(2)}) %collective-permute-start.5) | collective-permute-done | bytes 253984 | tf_op jit(solution)/shard_map/ppermute | solution.py:655
  51.7 3.7 %collective-permute-done.4.from_low = f32[2,31,8,128]{3,2,1,0:T(8,128)S(1)} collective-permute-done((f32[2,31,8,128]{3,2,1,0:T(8,128)S(1)}, f32[2,31,8,128]{3,2,1,0:T(8,128)S(1)}, u32[]{:S(2)}, u32[]{:S(2)}) %collective-permute-start.4) | collective-permute-done | bytes 253984 | tf_op jit(solution)/shard_map/ppermute | solution.py:655
  56.1 3.3 %collective-permute-start.6 = (f32[8,9,8,128]{3,2,1,0:T(8,128)S(1)}, f32[8,9,8,128]{3,2,1,0:T(8,128)S(1)}, u32[]{:S(2)}, u32[]{:S(2)}) collective-permute-start(f32[8,9,8,128]{3,2,1,0:T(8,128)S(1)} %get-tuple-element.37), channel_id=1, source_target_pairs={{0,1},{1,2},{2,3},{3,4},{4,5},{5,6},{6,7},{7,0},{8,9},{9,10},{10,1... | collective-permute-start | bytes 884744 | tf_op jit(solution)/shard_map/ppermute | solution.py:655
  59.4 3.7 %collective-permute-done.6.low_news = f32[8,9,8,128]{3,2,1,0:T(8,128)S(1)} collective-permute-done((f32[8,9,8,128]{3,2,1,0:T(8,128)S(1)}, f32[8,9,8,128]{3,2,1,0:T(8,128)S(1)}, u32[]{:S(2)}, u32[]{:S(2)}) %collective-permute-start.6) | collective-permute-done | bytes 294944 | tf_op jit(solution)/shard_map/ppermute | solution.py:655
  63.1 2.5 %collective-permute-done.7.high_news = f32[8,9,8,128]{3,2,1,0:T(8,128)S(1)} collective-permute-done((f32[8,9,8,128]{3,2,1,0:T(8,128)S(1)}, f32[8,9,8,128]{3,2,1,0:T(8,128)S(1)}, u32[]{:S(2)}, u32[]{:S(2)}) %collective-permute-start.7) | collective-permute-done | bytes 294944 | tf_op jit(solution)/shard_map/ppermute | solution.py:655
  65.5 6.3 %second_residual.1 = (f32[8,43,8,128]{3,2,1,0:T(8,128)S(1)}, f32[2,31,8,128]{3,2,1,0:T(8,128)S(1)}, f32[4,31,8,128]{3,2,1,0:T(8,128)S(1)}, f32[2,31,8,128]{3,2,1,0:T(8,128)S(1)}) custom-call(s32[4]{0:T(128)S(1)} %pad_add_fusion.place, f32[3,1,4,128]{3,2,1,0:T(4,128)S(1)} %copy-done.6, s32[8,32]{1,0:T(8,128)S(1)} %copy-done.3, ...), custom_call_target="tpu_custom_call" | custom-call | flops 100000000 | bytes 7232528 | tf_op jit(solution)/shard_map/second_residual/pallas_call | solution.py:376
  71.9 1.5 %collective-permute-start.8 = (f32[2,31,8,128]{3,2,1,0:T(8,128)S(1)}, f32[2,31,8,128]{3,2,1,0:T(8,128)S(1)}, u32[]{:S(2)}, u32[]{:S(2)}) collective-permute-start(f32[2,31,8,128]{3,2,1,0:T(8,128)S(1)} %get-tuple-element.42.high), channel_id=1, source_target_pairs={{0,8},{8,16},{16,24},{24,32},{32,40},{40,48},{48,56},{56,64},{64,7... | collective-permute-start | bytes 761864 | tf_op jit(solution)/shard_map/ppermute | solution.py:655
  73.4 6.2 %collective-permute-done.9.from_high = f32[2,31,8,128]{3,2,1,0:T(8,128)S(1)} collective-permute-done((f32[2,31,8,128]{3,2,1,0:T(8,128)S(1)}, f32[2,31,8,128]{3,2,1,0:T(8,128)S(1)}, u32[]{:S(2)}, u32[]{:S(2)}) %collective-permute-start.9) | collective-permute-done | bytes 253984 | tf_op jit(solution)/shard_map/ppermute | solution.py:655
  79.6 3.1 %collective-permute-done.8.from_low = f32[2,31,8,128]{3,2,1,0:T(8,128)S(1)} collective-permute-done((f32[2,31,8,128]{3,2,1,0:T(8,128)S(1)}, f32[2,31,8,128]{3,2,1,0:T(8,128)S(1)}, u32[]{:S(2)}, u32[]{:S(2)}) %collective-permute-start.8) | collective-permute-done | bytes 253984 | tf_op jit(solution)/shard_map/ppermute | solution.py:655
  82.7 10.7 %local_solve.3 = (f32[2,31,8,128]{3,2,1,0:T(8,128)S(1)}, f32[6,31,8,128]{3,2,1,0:T(8,128)S(1)}, f32[2,31,8,128]{3,2,1,0:T(8,128)S(1)}, f32[8,32,8,128]{3,2,1,0:T(8,128)}) custom-call(s32[4]{0:T(128)S(1)} %pad_add_fusion.place, f32[3,1,4,128]{3,2,1,0:T(4,128)S(1)} %copy-done.6, bf16[112,240]{1,0:T(8,128)(2,1)S(1)} %copy-done.11, ...), custom_call_target="tpu_custom_call" | custom-call | flops 1000000000 | bytes 4392976 | tf_op jit(solution)/shard_map/local_solve/pallas_call | solution.py:376
  94.8 5.0 %collective-permute-done.11.from_high = f32[2,31,8,128]{3,2,1,0:T(8,128)S(1)} collective-permute-done((f32[2,31,8,128]{3,2,1,0:T(8,128)S(1)}, f32[2,31,8,128]{3,2,1,0:T(8,128)S(1)}, u32[]{:S(2)}, u32[]{:S(2)}) %collective-permute-start.11) | collective-permute-done | bytes 253984 | tf_op jit(solution)/shard_map/ppermute | solution.py:655
  99.9 3.4 %collective-permute-done.10.from_low = f32[2,31,8,128]{3,2,1,0:T(8,128)S(1)} collective-permute-done((f32[2,31,8,128]{3,2,1,0:T(8,128)S(1)}, f32[2,31,8,128]{3,2,1,0:T(8,128)S(1)}, u32[]{:S(2)}, u32[]{:S(2)}) %collective-permute-start.10) | collective-permute-done | bytes 253984 | tf_op jit(solution)/shard_map/ppermute | solution.py:655
  104.0 3.0 %collective-permute-start.12 = (f32[8,2,8,128]{3,2,1,0:T(8,128)S(1)}, f32[8,2,8,128]{3,2,1,0:T(8,128)S(1)}, u32[]{:S(2)}, u32[]{:S(2)}) collective-permute-start(f32[8,2,8,128]{3,2,1,0:T(8,128)S(1)} %get-tuple-element.47), channel_id=1, source_target_pairs={{0,1},{1,2},{2,3},{3,4},{4,5},{5,6},{6,7},{7,0},{8,9},{9,10},{10,1... | collective-permute-start | bytes 196616 | tf_op jit(solution)/shard_map/ppermute | solution.py:655
  108.3 2.4 %collective-permute-done.13.high_news = f32[8,2,8,128]{3,2,1,0:T(8,128)S(1)} collective-permute-done((f32[8,2,8,128]{3,2,1,0:T(8,128)S(1)}, f32[8,2,8,128]{3,2,1,0:T(8,128)S(1)}, u32[]{:S(2)}, u32[]{:S(2)}) %collective-permute-start.13) | collective-permute-done | bytes 65568 | tf_op jit(solution)/shard_map/ppermute | solution.py:655
  110.7 1.7 %final_field.1 = f32[8,32,8,128]{3,2,1,0:T(8,128)} custom-call(s32[4]{0:T(128)S(1)} %pad_add_fusion.place, s32[8,32]{1,0:T(8,128)S(1)} %copy-done.3, f32[8,43,8,128]{3,2,1,0:T(8,128)S(1)} %get-tuple-element.39.field, f32[8,31,8,128]{3,2,1,0:T(8,128)S(1)} %get-tuple-element.46.correction, f32[8,2,8,128]{3,2,1,0:T(8,128)S(1)} %collective-permute-done.12.low_news, ...), custom_call_target="tpu_custom_call" | custom-call | flops 1000000 | bytes 3605520 | tf_op jit(solution)/shard_map/final_field/pallas_call | solution.py:376
  (39 shorter events, 6.0 us)
Async XLA Ops:
  0.6 11.2 %copy-start.2 = (bf16[128,192]{1,0:T(8,128)(2,1)S(1)}, bf16[128,192]{1,0:T(8,128)(2,1)}, u32[]{:S(2)}) copy-start(bf16[128,192]{1,0:T(8,128)(2,1)} %constant.31.clone.own_table) | copy-start | bytes 147460
  0.6 11.2 %copy-start.4 = (f32[8,8,128]{2,1,0:T(8,128)S(1)}, f32[8,8,128]{2,1,0:T(8,128)}, u32[]{:S(2)}) copy-start(f32[8,8,128]{2,1,0:T(8,128)} %constant.33.clone.plane_weights) | copy-start | bytes 98308
  0.7 11.2 %copy-start.5 = (bf16[64,192]{1,0:T(8,128)(2,1)S(1)}, bf16[64,192]{1,0:T(8,128)(2,1)}, u32[]{:S(2)}) copy-start(bf16[64,192]{1,0:T(8,128)(2,1)} %constant.32.clone.side_table) | copy-start | bytes 73732
  0.7 11.2 %copy-start.3 = (s32[8,32]{1,0:T(8,128)S(1)}, s32[8,32]{1,0:T(8,128)}, u32[]{:S(2)}) copy-start(s32[8,32]{1,0:T(8,128)} %outflow.11) | copy-start | bytes 3076
  2.9 6.6 %collective-permute-start = (f32[8,9,8,128]{3,2,1,0:T(8,128)}, f32[8,9,8,128]{3,2,1,0:T(8,128)S(1)}, u32[]{:S(2)}, u32[]{:S(2)}) collective-permute-start(f32[8,9,8,128]{3,2,1,0:T(8,128)} %get-tuple-element.26), channel_id=1, source_target_pairs={{0,1},{1,2},{2,3},{3,4},{4,5},{5,6},{6,7},{7,0},{8,9},{9,10},{10,1... | collective-permute-start | bytes 884744 | tf_op jit(solution)/shard_map/ppermute | solution.py:655
  5.5 6.4 %collective-permute-start.1 = (f32[8,9,8,128]{3,2,1,0:T(8,128)}, f32[8,9,8,128]{3,2,1,0:T(8,128)S(1)}, u32[]{:S(2)}, u32[]{:S(2)}) collective-permute-start(f32[8,9,8,128]{3,2,1,0:T(8,128)} %get-tuple-element.27), channel_id=1, source_target_pairs={{1,0},{2,1},{3,2},{4,3},{5,4},{6,5},{7,6},{0,7},{9,8},{10,9},{11,1... | collective-permute-start | bytes 884744 | tf_op jit(solution)/shard_map/ppermute | solution.py:655
  5.6 29.6 %copy-start.7 = (bf16[160,224]{1,0:T(8,128)(2,1)S(1)}, bf16[160,224]{1,0:T(8,128)(2,1)}, u32[]{:S(2)}) copy-start(bf16[160,224]{1,0:T(8,128)(2,1)} %constant.36.clone.backward) | copy-start | bytes 215044
  5.6 29.6 %copy-start.8 = (f32[112,128]{1,0:T(8,128)S(1)}, f32[112,128]{1,0:T(8,128)}, u32[]{:S(2)}) copy-start(f32[112,128]{1,0:T(8,128)} %constant.39.clone.third_values) | copy-start | bytes 172036
  5.6 29.6 %copy-start.9 = (f32[112,128]{1,0:T(8,128)S(1)}, f32[112,128]{1,0:T(8,128)}, u32[]{:S(2)}) copy-start(f32[112,128]{1,0:T(8,128)} %constant.38.clone.second_values) | copy-start | bytes 172036
  5.6 29.6 %copy-start.10 = (bf16[112,240]{1,0:T(8,128)(2,1)S(1)}, bf16[112,240]{1,0:T(8,128)(2,1)}, u32[]{:S(2)}) copy-start(bf16[112,240]{1,0:T(8,128)(2,1)} %constant.35.clone.forward_low) | copy-start | bytes 161284
  5.6 29.6 %copy-start.11 = (bf16[112,240]{1,0:T(8,128)(2,1)S(1)}, bf16[112,240]{1,0:T(8,128)(2,1)}, u32[]{:S(2)}) copy-start(bf16[112,240]{1,0:T(8,128)(2,1)} %constant.34.clone.forward_high) | copy-start | bytes 161284
  5.6 29.6 %copy-start.12 = (bf16[160,112]{1,0:T(8,128)(2,1)S(1)}, bf16[160,112]{1,0:T(8,128)(2,1)}, u32[]{:S(2)}) copy-start(bf16[160,112]{1,0:T(8,128)(2,1)} %constant.37.clone.backward_low) | copy-start | bytes 107524
  18.3 11.6 %collective-permute-start.3 = (f32[2,31,8,128]{3,2,1,0:T(8,128)S(1)}, f32[2,31,8,128]{3,2,1,0:T(8,128)S(1)}, u32[]{:S(2)}, u32[]{:S(2)}) collective-permute-start(f32[2,31,8,128]{3,2,1,0:T(8,128)S(1)} %get-tuple-element.30.low), channel_id=1, source_target_pairs={{8,0},{16,8},{24,16},{32,24},{40,32},{48,40},{56,48},{64,56},{72,6... | collective-permute-start | bytes 761864 | tf_op jit(solution)/shard_map/ppermute | solution.py:655
  24.6 10.6 %collective-permute-start.2 = (f32[2,31,8,128]{3,2,1,0:T(8,128)S(1)}, f32[2,31,8,128]{3,2,1,0:T(8,128)S(1)}, u32[]{:S(2)}, u32[]{:S(2)}) collective-permute-start(f32[2,31,8,128]{3,2,1,0:T(8,128)S(1)} %get-tuple-element.32.high), channel_id=1, source_target_pairs={{0,8},{8,16},{16,24},{24,32},{32,40},{40,48},{48,56},{56,64},{64,7... | collective-permute-start | bytes 761864 | tf_op jit(solution)/shard_map/ppermute | solution.py:655
  45.3 6.4 %collective-permute-start.5 = (f32[2,31,8,128]{3,2,1,0:T(8,128)S(1)}, f32[2,31,8,128]{3,2,1,0:T(8,128)S(1)}, u32[]{:S(2)}, u32[]{:S(2)}) collective-permute-start(f32[2,31,8,128]{3,2,1,0:T(8,128)S(1)} %get-tuple-element.33.low), channel_id=1, source_target_pairs={{8,0},{16,8},{24,16},{32,24},{40,32},{48,40},{56,48},{64,56},{72,6... | collective-permute-start | bytes 761864 | tf_op jit(solution)/shard_map/ppermute | solution.py:655
  45.7 9.7 %collective-permute-start.4 = (f32[2,31,8,128]{3,2,1,0:T(8,128)S(1)}, f32[2,31,8,128]{3,2,1,0:T(8,128)S(1)}, u32[]{:S(2)}, u32[]{:S(2)}) collective-permute-start(f32[2,31,8,128]{3,2,1,0:T(8,128)S(1)} %get-tuple-element.35.high), channel_id=1, source_target_pairs={{0,8},{8,16},{16,24},{24,32},{32,40},{40,48},{48,56},{56,64},{64,7... | collective-permute-start | bytes 761864 | tf_op jit(solution)/shard_map/ppermute | solution.py:655
  56.1 6.9 %collective-permute-start.6 = (f32[8,9,8,128]{3,2,1,0:T(8,128)S(1)}, f32[8,9,8,128]{3,2,1,0:T(8,128)S(1)}, u32[]{:S(2)}, u32[]{:S(2)}) collective-permute-start(f32[8,9,8,128]{3,2,1,0:T(8,128)S(1)} %get-tuple-element.37), channel_id=1, source_target_pairs={{0,1},{1,2},{2,3},{3,4},{4,5},{5,6},{6,7},{7,0},{8,9},{9,10},{10,1... | collective-permute-start | bytes 884744 | tf_op jit(solution)/shard_map/ppermute | solution.py:655
  59.4 6.1 %collective-permute-start.7 = (f32[8,9,8,128]{3,2,1,0:T(8,128)S(1)}, f32[8,9,8,128]{3,2,1,0:T(8,128)S(1)}, u32[]{:S(2)}, u32[]{:S(2)}) collective-permute-start(f32[8,9,8,128]{3,2,1,0:T(8,128)S(1)} %get-tuple-element.38), channel_id=1, source_target_pairs={{1,0},{2,1},{3,2},{4,3},{5,4},{6,5},{7,6},{0,7},{9,8},{10,9},{11,1... | collective-permute-start | bytes 884744 | tf_op jit(solution)/shard_map/ppermute | solution.py:655
  71.8 7.8 %collective-permute-start.9 = (f32[2,31,8,128]{3,2,1,0:T(8,128)S(1)}, f32[2,31,8,128]{3,2,1,0:T(8,128)S(1)}, u32[]{:S(2)}, u32[]{:S(2)}) collective-permute-start(f32[2,31,8,128]{3,2,1,0:T(8,128)S(1)} %get-tuple-element.40.low), channel_id=1, source_target_pairs={{8,0},{16,8},{24,16},{32,24},{40,32},{48,40},{56,48},{64,56},{72,6... | collective-permute-start | bytes 761864 | tf_op jit(solution)/shard_map/ppermute | solution.py:655
  71.9 10.8 %collective-permute-start.8 = (f32[2,31,8,128]{3,2,1,0:T(8,128)S(1)}, f32[2,31,8,128]{3,2,1,0:T(8,128)S(1)}, u32[]{:S(2)}, u32[]{:S(2)}) collective-permute-start(f32[2,31,8,128]{3,2,1,0:T(8,128)S(1)} %get-tuple-element.42.high), channel_id=1, source_target_pairs={{0,8},{8,16},{16,24},{24,32},{32,40},{40,48},{48,56},{56,64},{64,7... | collective-permute-start | bytes 761864 | tf_op jit(solution)/shard_map/ppermute | solution.py:655
  93.4 6.5 %collective-permute-start.11 = (f32[2,31,8,128]{3,2,1,0:T(8,128)S(1)}, f32[2,31,8,128]{3,2,1,0:T(8,128)S(1)}, u32[]{:S(2)}, u32[]{:S(2)}) collective-permute-start(f32[2,31,8,128]{3,2,1,0:T(8,128)S(1)} %get-tuple-element.43.low), channel_id=1, source_target_pairs={{8,0},{16,8},{24,16},{32,24},{40,32},{48,40},{56,48},{64,56},{72,6... | collective-permute-start | bytes 761864 | tf_op jit(solution)/shard_map/ppermute | solution.py:655
  93.5 9.8 %collective-permute-start.10 = (f32[2,31,8,128]{3,2,1,0:T(8,128)S(1)}, f32[2,31,8,128]{3,2,1,0:T(8,128)S(1)}, u32[]{:S(2)}, u32[]{:S(2)}) collective-permute-start(f32[2,31,8,128]{3,2,1,0:T(8,128)S(1)} %get-tuple-element.45.high), channel_id=1, source_target_pairs={{0,8},{8,16},{16,24},{24,32},{32,40},{40,48},{48,56},{56,64},{64,7... | collective-permute-start | bytes 761864 | tf_op jit(solution)/shard_map/ppermute | solution.py:655
  104.0 4.3 %collective-permute-start.12 = (f32[8,2,8,128]{3,2,1,0:T(8,128)S(1)}, f32[8,2,8,128]{3,2,1,0:T(8,128)S(1)}, u32[]{:S(2)}, u32[]{:S(2)}) collective-permute-start(f32[8,2,8,128]{3,2,1,0:T(8,128)S(1)} %get-tuple-element.47), channel_id=1, source_target_pairs={{0,1},{1,2},{2,3},{3,4},{4,5},{5,6},{6,7},{7,0},{8,9},{9,10},{10,1... | collective-permute-start | bytes 196616 | tf_op jit(solution)/shard_map/ppermute | solution.py:655
  107.0 3.7 %collective-permute-start.13 = (f32[8,2,8,128]{3,2,1,0:T(8,128)S(1)}, f32[8,2,8,128]{3,2,1,0:T(8,128)S(1)}, u32[]{:S(2)}, u32[]{:S(2)}) collective-permute-start(f32[8,2,8,128]{3,2,1,0:T(8,128)S(1)} %get-tuple-element.48), channel_id=1, source_target_pairs={{1,0},{2,1},{3,2},{4,3},{5,4},{6,5},{7,6},{0,7},{9,8},{10,9},{11,1... | collective-permute-start | bytes 196616 | tf_op jit(solution)/shard_map/ppermute | solution.py:655
  (3 other events, 33.6 us)
